TPU v7x, 32 devices: a whole 2x2x4 slice. The times are simulated.
32 devices in a mesh: grp: 2 (over y), dp: 4 (over z), feat: 2 (over x), qry: 2 (over core).
Axes of the slice: x: 2, y: 2, z: 4, core: 2. Of those that a mesh axis runs over, the one named last changes fastest.
Arguments:
- train_grads: bfloat16 [10240, 4096], P(('grp', 'dp'), 'feat'), parts along dimension 0, may hold values from -6 to 6
- queries: bfloat16 [4, 96, 4096], P('dp', 'qry', 'feat'), may hold values from -0.09375 to 0.09375
- loss_weights: float32 [10240], P(('grp', 'dp', 'feat')), parts along dimension 0, may hold values from 0.2 to 1
Outputs:
- scores: float32 [4, 96, 10240], P(None, 'qry', ('grp', 'dp', 'feat')), parts along dimension 2
There are 2 independent parts, one for each index of `grp`. A program takes and returns all parts, laid end to end along the dimension named above; an argument that names none is the same for every part. Nothing has to cross between parts.
All inputs are finite; a program needn't handle non-finite values.
Results may differ from a plain program's by a relative error of at most 0.0003.
Values may be sent and summed in bfloat16 or wider, within the bound.
A program may use at most 64 MiB of HBM per device.

v0:
```python
import jax
import jax.numpy as jnp
from jax import lax
from jax.sharding import PartitionSpec as P


def from_behind(value, axis, by):
    peers = lax.axis_size(axis)
    return lax.ppermute(value, axis, [(i, (i + by) % peers) for i in range(peers)])


def score_blocks(table_rows, first_block):
    members = lax.axis_size("dp")
    position = lax.axis_index("dp")
    width_rows = table_rows.shape[0]
    block_rows = first_block.shape[0]

    def product(current):
        return lax.dot_general(
            current, table_rows, (((1,), (1,)), ((), ())), preferred_element_type=jnp.float32
        )

    def deposit(score_table, current, anchor):
        return lax.dynamic_update_slice(score_table, product(current)[None], (anchor, 0, 0))

    score_table = jnp.zeros((members, block_rows, width_rows), jnp.float32)
    score_table = deposit(score_table, first_block, position)

    def advance(offset, carried):
        score_table, current = carried
        current = from_behind(current, "dp", 1)
        anchor = (position - offset) % members
        return (deposit(score_table, current, anchor), current)

    score_table, current = lax.fori_loop(1, members, advance, (score_table, first_block))
    return score_table


def local(train_grads, queries, loss_weights):
    local_block = queries[0]
    full_rows = lax.all_to_all(train_grads, "feat", split_axis=0, concat_axis=1, tiled=True)
    full_block = lax.all_gather(local_block, "feat", axis=1, tiled=True)
    totals = score_blocks(full_rows, full_block)
    return totals * loss_weights[None, None, :]


def solution(mesh):
    in_specs = (P(("grp", "dp"), "feat"), P("dp", "qry", "feat"), P(("grp", "dp", "feat")))
    out_specs = P(None, "qry", ("grp", "dp", "feat"))
    return jax.shard_map(local, mesh=mesh, in_specs=in_specs, out_specs=out_specs, check_vma=False)
```

profile of v0, /device:TPU:0, one launch (start us, length us, event | category | flops | bytes accessed | tf_op | source)
XLA Modules:
  0.0 136.6 jit_solution(3804063809409410987)
XLA Ops:
  0.0 0.0 copy-start
  0.0 6.1 %all-to-all-start = ((bf16[2,640,2048]{2,1,0:T(8,128)(2,1)}), bf16[2,640,2048]{2,1,0:T(8,128)(2,1)}, u32[]{:S(2)}, u32[]{:S(2)}) async-start(bf16[2,640,2048]{2,1,0:T(8,128)(2,1)} %bitcast.26), calls=%async_computation | async-start | bytes 10485760 | tf_op jit(solution)/shard_map/all_to_all | solution.py:41
  6.1 0.0 copy-done
  6.1 64.2 %all-gather = bf16[1,48,4096]{2,1,0:T(8,128)(2,1)S(1)} all-gather(bf16[1,48,2048]{2,1,0:T(8,128)(2,1)S(1)} %copy-done), channel_id=2, replica_groups=mesh['grp'=2,'dp'=4,'feat'=2,'qry'=2] {'feat'}, dimensions={2}, use_global_device_ids=true | all-gather | bytes 589824 | tf_op jit(solution)/shard_map/all_gather | solution.py:42
  70.3 0.0 all-to-all-done
  70.3 7.8 %copy.5 = bf16[2,640,2048]{1,2,0:T(8,128)(2,1)} copy(bf16[2,640,2048]{2,1,0:T(8,128)(2,1)} %all-to-all-done) | data formatting | bytes 10485760 | tf_op jit(solution)/shard_map/all_to_all | solution.py:41
  78.1 8.0 %copy.6 = bf16[640,4096]{1,0:T(8,128)(2,1)} copy(bf16[640,4096]{0,1:T(8,128)(2,1)} %bitcast.24) | data formatting | bytes 10485760 | tf_op jit(solution)/shard_map/while | solution.py:35
  86.2 3.4 %fusion.1 = f32[4,48,640]{2,1,0:T(8,128)S(1)} fusion(f32[4,48,640]{2,1,0:T(8,128)S(1)} %broadcast_in_dim.17, s32[]{:T(128)S(6)} %select_n.33, bf16[640,4096]{0,1:T(8,128)(2,1)} %bitcast.25, bf16[1,48,4096]{2,1,0:T(8,128)(2,1)S(1)} %all-gather), kind=kOutput, calls=%fused_computation.3 | convolution fusion | flops 251658240 | bytes 5758980 | tf_op jit(solution)/shard_map/dot_general | solution.py:19
  89.6 0.0 copy-start.1
  89.6 46.2 %while.17 = (s32[]{:T(128)}, f32[4,48,640]{2,1,0:T(8,128)S(1)}, bf16[48,4096]{1,0:T(8,128)(2,1)S(1)}, bf16[640,4096]{1,0:T(8,128)(2,1)}, s32[]{:T(128)}, /*index=5*/s32[]{:T(128)}, s32[]{:T(128)}, s32[]{:T(128)}, s32[]{:T(128)}) while((s32[]{:T(128)}, f32[4,48,640]{2,1,0:T(8,128)S(1)}, bf16[48,4096]{1,0:T(8,128)(2,1)S(1)}, ...), condition=%wide.region_1.2_spmd, body=%wide.region_0.1_spmd.sunk | while | flops 251658256 | bytes 8118564 | solution.py:35
  89.6 1.9 %collective-permute-start = (bf16[48,4096]{1,0:T(8,128)(2,1)S(1)}, bf16[48,4096]{1,0:T(8,128)(2,1)S(1)}, u32[]{:S(2)}, u32[]{:S(2)}) collective-permute-start(bf16[48,4096]{1,0:T(8,128)(2,1)S(1)} %get-tuple-element.196), channel_id=1, source_target_pairs={{0,4},{4,8},{8,12},{12,0},{1,5},{5,9},{9,13},{13,1},{2,6},{6,10},{... | collective-permute-start | bytes 1179656 | tf_op jit(solution)/shard_map/while/body/eval_jaxpr/ppermute | solution.py:9
  91.5 10.3 %collective-permute-done = bf16[48,4096]{1,0:T(8,128)(2,1)S(1)} collective-permute-done((bf16[48,4096]{1,0:T(8,128)(2,1)S(1)}, bf16[48,4096]{1,0:T(8,128)(2,1)S(1)}, u32[]{:S(2)}, u32[]{:S(2)}) %collective-permute-start) | collective-permute-done | bytes 393248 | tf_op jit(solution)/shard_map/while/body/eval_jaxpr/ppermute | solution.py:9
  101.8 4.2 %fusion.11 = f32[4,48,640]{2,1,0:T(8,128)S(1)} fusion(f32[4,48,640]{2,1,0:T(8,128)S(1)} %get-tuple-element.195, s32[]{:T(128)S(6)} %select_n.37, bf16[48,4096]{1,0:T(8,128)(2,1)S(1)} %collective-permute-done, bf16[640,4096]{1,0:T(8,128)(2,1)} %get-tuple-element.206), kind=kOutput, calls=%fused_computation.1.clone.1 | convolution fusion | flops 251658240 | bytes 5758980 | tf_op jit(solution)/shard_map/while/body/eval_jaxpr/dot_general | solution.py:19
  106.0 0.1 collective-permute-start
  106.1 11.1 %collective-permute-done = bf16[48,4096]{1,0:T(8,128)(2,1)S(1)} collective-permute-done((bf16[48,4096]{1,0:T(8,128)(2,1)S(1)}, bf16[48,4096]{1,0:T(8,128)(2,1)S(1)}, u32[]{:S(2)}, u32[]{:S(2)}) %collective-permute-start) | collective-permute-done | bytes 393248 | tf_op jit(solution)/shard_map/while/body/eval_jaxpr/ppermute | solution.py:9
  117.2 4.2 %fusion.11 = f32[4,48,640]{2,1,0:T(8,128)S(1)} fusion(f32[4,48,640]{2,1,0:T(8,128)S(1)} %get-tuple-element.195, s32[]{:T(128)S(6)} %select_n.37, bf16[48,4096]{1,0:T(8,128)(2,1)S(1)} %collective-permute-done, bf16[640,4096]{1,0:T(8,128)(2,1)} %get-tuple-element.206), kind=kOutput, calls=%fused_computation.1.clone.1 | convolution fusion | flops 251658240 | bytes 5758980 | tf_op jit(solution)/shard_map/while/body/eval_jaxpr/dot_general | solution.py:19
  121.4 0.1 collective-permute-start
  121.5 10.2 %collective-permute-done = bf16[48,4096]{1,0:T(8,128)(2,1)S(1)} collective-permute-done((bf16[48,4096]{1,0:T(8,128)(2,1)S(1)}, bf16[48,4096]{1,0:T(8,128)(2,1)S(1)}, u32[]{:S(2)}, u32[]{:S(2)}) %collective-permute-start) | collective-permute-done | bytes 393248 | tf_op jit(solution)/shard_map/while/body/eval_jaxpr/ppermute | solution.py:9
  131.7 4.1 %fusion.11 = f32[4,48,640]{2,1,0:T(8,128)S(1)} fusion(f32[4,48,640]{2,1,0:T(8,128)S(1)} %get-tuple-element.195, s32[]{:T(128)S(6)} %select_n.37, bf16[48,4096]{1,0:T(8,128)(2,1)S(1)} %collective-permute-done, bf16[640,4096]{1,0:T(8,128)(2,1)} %get-tuple-element.206), kind=kOutput, calls=%fused_computation.1.clone.1 | convolution fusion | flops 251658240 | bytes 5758980 | tf_op jit(solution)/shard_map/while/body/eval_jaxpr/dot_general | solution.py:19
  135.8 0.0 copy-done.1
  135.8 0.8 broadcast_multiply_fusion
  (4 shorter events, 0.1 us)
Async XLA Ops:
  0.0 6.1 %copy-start = (bf16[1,48,2048]{2,1,0:T(8,128)(2,1)S(1)}, bf16[1,48,2048]{2,1,0:T(8,128)(2,1)}, u32[]{:S(2)}) copy-start(bf16[1,48,2048]{2,1,0:T(8,128)(2,1)} %param.6) | copy-start | bytes 589828
  0.0 70.3 %all-to-all-start = ((bf16[2,640,2048]{2,1,0:T(8,128)(2,1)}), bf16[2,640,2048]{2,1,0:T(8,128)(2,1)}, u32[]{:S(2)}, u32[]{:S(2)}) async-start(bf16[2,640,2048]{2,1,0:T(8,128)(2,1)} %bitcast.26), calls=%async_computation | async-start | bytes 10485760 | tf_op jit(solution)/shard_map/all_to_all | solution.py:41
  89.6 46.2 %copy-start.1 = (f32[640]{0:T(1024)S(1)}, f32[640]{0:T(1024)}, u32[]{:S(2)}) copy-start(f32[640]{0:T(1024)} %param.7) | copy-start | bytes 7684
  89.6 12.2 %collective-permute-start = (bf16[48,4096]{1,0:T(8,128)(2,1)S(1)}, bf16[48,4096]{1,0:T(8,128)(2,1)S(1)}, u32[]{:S(2)}, u32[]{:S(2)}) collective-permute-start(bf16[48,4096]{1,0:T(8,128)(2,1)S(1)} %get-tuple-element.196), channel_id=1, source_target_pairs={{0,4},{4,8},{8,12},{12,0},{1,5},{5,9},{9,13},{13,1},{2,6},{6,10},{... | collective-permute-start | bytes 1179656 | tf_op jit(solution)/shard_map/while/body/eval_jaxpr/ppermute | solution.py:9
  106.0 11.2 %collective-permute-start = (bf16[48,4096]{1,0:T(8,128)(2,1)S(1)}, bf16[48,4096]{1,0:T(8,128)(2,1)S(1)}, u32[]{:S(2)}, u32[]{:S(2)}) collective-permute-start(bf16[48,4096]{1,0:T(8,128)(2,1)S(1)} %get-tuple-element.196), channel_id=1, source_target_pairs={{0,4},{4,8},{8,12},{12,0},{1,5},{5,9},{9,13},{13,1},{2,6},{6,10},{... | collective-permute-start | bytes 1179656 | tf_op jit(solution)/shard_map/while/body/eval_jaxpr/ppermute | solution.py:9
  121.4 10.3 %collective-permute-start = (bf16[48,4096]{1,0:T(8,128)(2,1)S(1)}, bf16[48,4096]{1,0:T(8,128)(2,1)S(1)}, u32[]{:S(2)}, u32[]{:S(2)}) collective-permute-start(bf16[48,4096]{1,0:T(8,128)(2,1)S(1)} %get-tuple-element.196), channel_id=1, source_target_pairs={{0,4},{4,8},{8,12},{12,0},{1,5},{5,9},{9,13},{13,1},{2,6},{6,10},{... | collective-permute-start | bytes 1179656 | tf_op jit(solution)/shard_map/while/body/eval_jaxpr/ppermute | solution.py:9
where the time goes:
time: 137 us
  blocking collectives  64.2 us (47%)
  waiting for transfers between devices  31.5 us (23%)
  local copies, waits for them, and re-layouts  16 us (12%)
  matrix products  15.9 us (12%)
  starting transfers between devices  8.09 us (6%)
    all_gather x1, blocking collectives, local(): full_block = lax.all_gather(local_block, 'feat', axis=1, tiled=True)  64.2 us
    ppermute x3, waiting for transfers between devices, from_behind(): lax.ppermute(value, axis, [(i, (i + by) % peers) for i in range(peers)])  31.5 us
    dot_general x4, matrix products, product(): lax.dot_general(current, table_rows, (((1,), (1,)), ((), ())), preferred_...  15.9 us
    while x1, local copies, waits for them, and re-layouts, score_blocks(): lax.fori_loop(1, members, advance, (score_table, first_block))  8.01 us
    all_to_all x1, local copies, waits for them, and re-layouts, local(): lax.all_to_all(train_grads, 'feat', split_axis=0, concat_axis=1, tiled=True)  7.84 us
    all_to_all x1, starting transfers between devices, local(): lax.all_to_all(train_grads, 'feat', split_axis=0, concat_axis=1, tiled=True)  6.09 us
  transfers between devices with their start and end apart: 4, of which 3 were waited for; matrix products, arithmetic and copies ran while one was open for 0% of the time, Pallas kernels for 0%

commit v1 on v0

v1 whole, which is shorter than its diff:
```python
import functools

import jax
import jax.numpy as jnp
from jax import lax
from jax.experimental import pallas as pl
from jax.experimental.pallas import tpu as pltpu
from jax.sharding import PartitionSpec as P

MESH = pl.DeviceIdType.MESH


def partner(me, step, size):
    if size & (size - 1):
        return lax.rem(me + step, size)
    out = me
    bit = 1
    while bit < size:
        both = (me // bit) % 2
        flip = (step // bit) % 2
        out = out + bit * flip * (1 - 2 * both)
        bit *= 2
    return out


def source(me, step, size):
    if size & (size - 1):
        return lax.rem(me - step + size, size)
    return partner(me, step, size)


def kernel(
    sizes, train_hbm, query_hbm, out_ref, train, blocks, sent, received,
    train_sem, own_sem, z_send, z_recv, y_send, y_recv, x_send, x_recv,
):
    G, D, F = sizes
    g, d, f = lax.axis_index("grp"), lax.axis_index("dp"), lax.axis_index("feat")
    rows = out_ref.shape[2]
    width = blocks.shape[3]

    barrier = pltpu.get_barrier_semaphore()
    for s in range(1, D):
        pl.semaphore_signal(barrier, inc=1, device_id={"dp": partner(d, s, D)}, device_id_type=MESH)
    for k in range(1, G):
        pl.semaphore_signal(barrier, inc=1, device_id={"grp": lax.rem(g + k, G)}, device_id_type=MESH)
    for k in range(1, F):
        pl.semaphore_signal(barrier, inc=1, device_id={"feat": lax.rem(f + k, F)}, device_id_type=MESH)

    own = [
        pltpu.make_async_copy(query_hbm.at[0, :, pl.ds(p * width, width)], blocks.at[d, p], own_sem.at[p])
        for p in range(G)
    ]
    for copy in own:
        copy.start()
    order = [lax.rem(f + k, F) for k in list(range(1, F)) + [0]]
    loads = []
    for k in range(F):
        for p in range(G):
            at = (pl.ds(pl.multiple_of(order[k] * rows, rows), rows), pl.ds(p * width, width))
            loads.append(pltpu.make_async_copy(train_hbm.at[at], train.at[at], train_sem.at[k, p]))
            loads[-1].start()

    pl.semaphore_wait(barrier, (D - 1) + (G - 1) + (F - 1))

    def across(s):
        to = partner(d, s, D)
        return pltpu.make_async_remote_copy(
            src_ref=query_hbm.at[0, :, pl.ds(pl.multiple_of(g * width, width), width)],
            dst_ref=blocks.at[d, g],
            send_sem=z_send.at[s], recv_sem=z_recv.at[s],
            device_id={"dp": to}, device_id_type=MESH,
        )

    def arrived(s):
        b = source(d, s, D)
        return pltpu.make_async_remote_copy(
            src_ref=blocks.at[b, g], dst_ref=blocks.at[b, g],
            send_sem=z_send.at[s], recv_sem=z_recv.at[s],
            device_id={"dp": partner(d, s, D)}, device_id_type=MESH,
        )

    def forward(s, k):
        b = source(d, s, D)
        return pltpu.make_async_remote_copy(
            src_ref=blocks.at[b, g], dst_ref=blocks.at[b, g],
            send_sem=y_send.at[s, k], recv_sem=y_recv.at[s, k],
            device_id={"grp": lax.rem(g + k, G)}, device_id_type=MESH,
        )

    def forwarded(s, k):
        b = source(d, s, D)
        at = lax.rem(g - k + G, G)
        return pltpu.make_async_remote_copy(
            src_ref=blocks.at[b, at], dst_ref=blocks.at[b, at],
            send_sem=y_send.at[s, k], recv_sem=y_recv.at[s, k],
            device_id={"grp": lax.rem(g + k, G)}, device_id_type=MESH,
        )

    def give(s, k):
        return pltpu.make_async_remote_copy(
            src_ref=sent.at[k - 1, s], dst_ref=received.at[k - 1, partner_slot(s)],
            send_sem=x_send.at[s, k - 1], recv_sem=x_recv.at[s, k - 1],
            device_id={"feat": lax.rem(f + k, F)}, device_id_type=MESH,
        )

    def partner_slot(s):
        return s

    def product(b, k):
        at = pl.ds(pl.multiple_of(order[k] * rows, rows), rows)
        total = None
        for p in range(G):
            term = lax.dot_general(
                blocks[b, p], train[at, pl.ds(p * width, width)],
                (((1,), (1,)), ((), ())), preferred_element_type=jnp.float32,
            )
            total = term if total is None else total + term
        return total

    for s in range(1, D):
        across(s).start()

    for copy in own:
        copy.wait()

    for k in range(1, F):
        for p in range(G):
            loads[(k - 1) * G + p].wait()
        sent[k - 1, 0] = product(d, k - 1)
        give(0, k).start()

    def pass_on(s):
        arrived(s).wait_recv()
        for k in range(1, G):
            forward(s, k).start()

    if D > 1:
        pass_on(1)
    for p in range(G):
        loads[(F - 1) * G + p].wait()
    out_ref[d] = product(d, F - 1)

    def step(s, last):
        b = source(d, s, D)
        if not last:
            pass_on(s + 1)
        for k in range(1, G):
            forwarded(s, k).wait_recv()
        for k in range(1, F):
            sent[k - 1, s] = product(b, k - 1)
            give(s, k).start()
        out_ref[b] = product(b, F - 1)

    if D > 2:
        lax.fori_loop(1, D - 1, lambda s, c: (step(s, False), c)[1], 0)
    if D > 1:
        step(D - 1, True)

    def finish(s, c):
        b = source(d, s, D)
        for k in range(1, F):
            give(s, k).wait_recv()
            out_ref[b] += received[k - 1, s]
        return c

    lax.fori_loop(0, D, finish, 0)

    def drain(s, c):
        across(s).wait_send()
        for k in range(1, G):
            forward(s, k).wait_send()
        return c

    lax.fori_loop(1, D, drain, 0)

    def drain_given(s, c):
        for k in range(1, F):
            give(s, k).wait_send()
        return c

    lax.fori_loop(0, D, drain_given, 0)


def local(sizes, train_grads, queries, loss_weights):
    G, D, F = sizes
    total_rows, features = train_grads.shape
    rows = total_rows // F
    width = features // G
    held = queries.shape[1]
    sums = pl.pallas_call(
        functools.partial(kernel, sizes),
        out_shape=jax.ShapeDtypeStruct((D, held, rows), jnp.float32),
        in_specs=[pl.BlockSpec(memory_space=pl.ANY)] * 2,
        out_specs=pl.BlockSpec(memory_space=pltpu.VMEM),
        scratch_shapes=[
            pltpu.VMEM((total_rows, features), jnp.bfloat16),
            pltpu.VMEM((D, G, held, width), jnp.bfloat16),
            pltpu.VMEM((F - 1, D, held, rows), jnp.float32),
            pltpu.VMEM((F - 1, D, held, rows), jnp.float32),
            pltpu.SemaphoreType.DMA((F, G)),
            pltpu.SemaphoreType.DMA((G,)),
            pltpu.SemaphoreType.DMA((D,)),
            pltpu.SemaphoreType.DMA((D,)),
            pltpu.SemaphoreType.DMA((D, G)),
            pltpu.SemaphoreType.DMA((D, G)),
            pltpu.SemaphoreType.DMA((D, F - 1)),
            pltpu.SemaphoreType.DMA((D, F - 1)),
        ],
        compiler_params=pltpu.CompilerParams(
            collective_id=0, has_side_effects=True, vmem_limit_bytes=56 * 1024 * 1024
        ),
        cost_estimate=pl.CostEstimate(
            flops=2 * D * held * total_rows * features,
            bytes_accessed=2 * total_rows * features + 4 * D * held * rows,
            transcendentals=0,
        ),
    )(train_grads, queries)
    return sums * loss_weights[None, None, :]


def solution(mesh):
    sizes = tuple(mesh.shape[axis] for axis in ("grp", "dp", "feat"))
    in_specs = (P(("grp", "dp"), "feat"), P("dp", "qry", "feat"), P(("grp", "dp", "feat")))
    out_specs = P(None, "qry", ("grp", "dp", "feat"))
    return jax.shard_map(
        functools.partial(local, sizes), mesh=mesh, in_specs=in_specs, out_specs=out_specs, check_vma=False
    )
```

time: 137 us -> 29.4 us (0.21)
  blocking collectives: 64.2 us -> 0 us
  waiting for transfers between devices: 31.5 us -> 0 us
  Pallas kernels: 0 us -> 27.4 us
  local copies, waits for them, and re-layouts: 16 us -> 0.01 us
  matrix products: 15.9 us -> 0 us
  starting transfers between devices: 8.09 us -> 0 us
    all_gather x1 -> x0, blocking collectives: 64.2 us -> none  [local(): full_block = lax.all_gather(local_block, 'feat', axis=1, tiled=True)]
    ppermute x3 -> x0, waiting for transfers between devices: 31.5 us -> none  [from_behind(): lax.ppermute(value, axis, [(i, (i + by) % peers) for i in range(peers)])]
    pallas_call x0 -> x1, Pallas kernels: none -> 27.4 us  [local(): pl.pallas_call(functools.partial(kernel, sizes), out_shape=jax.ShapeDtype...]
    dot_general x4 -> x0, matrix products: 15.9 us -> none  [product(): lax.dot_general(current, table_rows, (((1,), (1,)), ((), ())), preferred_...]
    while x4 -> x0, local copies, waits for them, and re-layouts: 8.09 us -> none  [the longest x1 8.01 us: score_blocks(): lax.fori_loop(1, members, advance, (score_table, first_block))]
    all_to_all x1 -> x0, local copies, waits for them, and re-layouts: 7.84 us -> none  [local(): lax.all_to_all(train_grads, 'feat', split_axis=0, concat_axis=1, tiled=True)]
    all_to_all x1 -> x0, starting transfers between devices: 6.09 us -> none  [local(): lax.all_to_all(train_grads, 'feat', split_axis=0, concat_axis=1, tiled=True)]
    ppermute x3 -> x0, starting transfers between devices: 2 us -> none  [from_behind(): lax.ppermute(value, axis, [(i, (i + by) % peers) for i in range(peers)])]
  transfers between devices with their start and end apart: 4 -> 0, of which waited for: 3 -> 0; matrix products, arithmetic and copies ran while one was open for 0% -> 0% of each run, Pallas kernels for 0% -> 0%
where the time goes in v1:
time: 29.4 us; the launch traced here: 29.2 us
  Pallas kernels  27.4 us (93%)
  other arithmetic  1.84 us (6%)
    pallas_call x1, Pallas kernels, local(): pl.pallas_call(functools.partial(kernel, sizes), out_shape=jax.ShapeDtype...  27.4 us
    mul x1, other arithmetic, local(): return sums * loss_weights[None, None, :]  1.84 us

profile of v1, /device:TPU:0, one launch (start us, length us, event | category | flops | bytes accessed | tf_op | source)
XLA Modules:
  0.0 29.2 jit_solution(17648563245780845739)
XLA Ops:
  0.0 0.0 copy-start
  0.0 27.4 %shard_map.37 = f32[4,48,640]{2,1,0:T(8,128)} custom-call(bf16[1280,2048]{1,0:T(8,128)(2,1)} %train_hbm.1, bf16[1,48,2048]{2,1,0:T(8,128)(2,1)} %query_hbm.1), custom_call_target="tpu_custom_call" | custom-call | flops 1006632960 | bytes 5734400 | tf_op jit(solution)/shard_map/pallas_call | solution.py:190
  27.4 0.0 copy-done
  27.4 1.8 %broadcast_multiply_fusion = f32[4,48,640]{2,1,0:T(8,128)} fusion(f32[4,48,640]{2,1,0:T(8,128)} %shard_map.37, f32[640]{0:T(1024)S(1)} %copy-done), kind=kLoop, calls=%fused_computation | loop fusion | flops 122880 | bytes 985600 | tf_op jit(solution)/shard_map/mul | solution.py:218
Async XLA Ops:
  0.0 27.4 %copy-start = (f32[640]{0:T(1024)S(1)}, f32[640]{0:T(1024)}, u32[]{:S(2)}) copy-start(f32[640]{0:T(1024)} %param.5) | copy-start | bytes 7684

commit v2 on v1

v2 whole, which is shorter than its diff:
```python
import functools

import jax
import jax.numpy as jnp
from jax import lax
from jax.experimental import pallas as pl
from jax.experimental.pallas import tpu as pltpu
from jax.sharding import PartitionSpec as P

MESH = pl.DeviceIdType.MESH


def arrival(me, j, size):
    both = jnp.minimum(me, size - 1 - me)
    left_longer = (2 * me) // size
    step = jnp.where(j <= 2 * both, (j + 1) // 2, j - both)
    to_left = jnp.where(j <= 2 * both, j % 2, left_longer)
    return me + step * (1 - 2 * to_left), to_left


def kernel(
    sizes, parts, train_hbm, query_hbm, out_ref, train, blocks, sent, received,
    train_sem, own_sem, first_send, z_send, z_recv, y_send, y_recv, x_send, x_recv,
):
    G, D, F = sizes
    g, d, f = lax.axis_index("grp"), lax.axis_index("dp"), lax.axis_index("feat")
    rows = out_ref.shape[2]
    width = blocks.shape[3]
    pieces = G * parts
    has_left, has_right = d > 0, d < D - 1

    barrier = pltpu.get_barrier_semaphore()
    for there, by in ((has_left, -1), (has_right, 1)):
        @pl.when(there)
        def _():
            pl.semaphore_signal(barrier, inc=1, device_id={"dp": d + by}, device_id_type=MESH)
    for k in range(1, G):
        pl.semaphore_signal(barrier, inc=1, device_id={"grp": lax.rem(g + k, G)}, device_id_type=MESH)
    for k in range(1, F):
        pl.semaphore_signal(barrier, inc=1, device_id={"feat": lax.rem(f + k, F)}, device_id_type=MESH)

    own = [
        pltpu.make_async_copy(query_hbm.at[0, :, pl.ds(p * width, width)], blocks.at[d, p], own_sem.at[p])
        for p in range(pieces)
    ]
    for copy in own:
        copy.start()
    order = [lax.rem(f + k, F) for k in list(range(1, F)) + [0]]
    loads = []
    for k in range(F):
        for p in range(G):
            cols = pl.ds(p * width * parts, width * parts)
            at = (pl.ds(pl.multiple_of(order[k] * rows, rows), rows), cols)
            loads.append(pltpu.make_async_copy(train_hbm.at[at], train.at[at], train_sem.at[k, p]))
            loads[-1].start()

    pl.semaphore_wait(barrier, has_left.astype(jnp.int32) + has_right.astype(jnp.int32) + (G - 1) + (F - 1))

    def first(by, c):
        at = pl.multiple_of((g * parts + c) * width, width)
        return pltpu.make_async_remote_copy(
            src_ref=query_hbm.at[0, :, pl.ds(at, width)], dst_ref=blocks.at[d, g * parts + c],
            send_sem=first_send.at[(by + 1) // 2, c], recv_sem=z_recv.at[d, c],
            device_id={"dp": d + by}, device_id_type=MESH,
        )

    def along(b, by, c):
        at = blocks.at[b, g * parts + c]
        return pltpu.make_async_remote_copy(
            src_ref=at, dst_ref=at, send_sem=z_send.at[b, c], recv_sem=z_recv.at[b, c],
            device_id={"dp": d + by}, device_id_type=MESH,
        )

    def over(b, k, c):
        at = blocks.at[b, g * parts + c]
        return pltpu.make_async_remote_copy(
            src_ref=at, dst_ref=at, send_sem=y_send.at[b, k, c], recv_sem=y_recv.at[b, k, c],
            device_id={"grp": lax.rem(g + k, G)}, device_id_type=MESH,
        )

    def over_here(b, k, c):
        at = blocks.at[b, lax.rem(g - k + G, G) * parts + c]
        return pltpu.make_async_remote_copy(
            src_ref=at, dst_ref=at, send_sem=y_send.at[b, k, c], recv_sem=y_recv.at[b, k, c],
            device_id={"grp": lax.rem(g + k, G)}, device_id_type=MESH,
        )

    def give(b, k):
        return pltpu.make_async_remote_copy(
            src_ref=sent.at[k - 1, b], dst_ref=received.at[k - 1, b],
            send_sem=x_send.at[b, k - 1], recv_sem=x_recv.at[b, k - 1],
            device_id={"feat": lax.rem(f + k, F)}, device_id_type=MESH,
        )

    def product(of, k):
        at = pl.ds(pl.multiple_of(order[k] * rows, rows), rows)
        total = None
        for p in range(pieces):
            term = lax.dot_general(
                of(p), train[at, pl.ds(p * width, width)],
                (((1,), (1,)), ((), ())), preferred_element_type=jnp.float32,
            )
            total = term if total is None else total + term
        return total

    def send_products(b):
        for k in range(1, F):
            sent[k - 1, b] = product(lambda p: blocks[b, p], k - 1)
            give(b, k).start()

    def pass_on(j, c):
        b, to_left = arrival(d, j, D)
        along(b, 1, c).wait_recv()
        by = 2 * to_left - 1
        onward = jnp.logical_and(d + by >= 0, d + by < D)

        @pl.when(onward)
        def _():
            along(b, by, c).start()
        for k in range(1, G):
            over(b, k, c).start()

    def use(j):
        b, _ = arrival(d, j, D)
        for c in range(parts):
            for k in range(1, G):
                over_here(b, k, c).wait_recv()
        send_products(b)

    for c in range(parts):
        for there, by in ((has_left, -1), (has_right, 1)):
            @pl.when(there)
            def _():
                first(by, c).start()

    for copy in own:
        copy.wait()
    for load in loads[: (F - 1) * G]:
        load.wait()
    send_products(d)

    def step(j):
        for c in range(parts):
            pass_on(j + 1, c)
        use(j)

    if D > 1:
        for c in range(parts):
            pass_on(1, c)
        if D > 2:
            lax.fori_loop(1, D - 1, lambda j, carry: (step(j), carry)[1], 0)
        use(D - 1)

    for load in loads[(F - 1) * G :]:
        load.wait()

    many = max(n for n in (1, 2, 3, 4) if D % n == 0)

    def keep(i, carry):
        at = pl.ds(i * many, many)
        held = out_ref.shape[1]
        total = product(lambda p: blocks[at, p].reshape(many * held, width), F - 1)
        out_ref[at] = total.reshape(many, held, rows)
        return carry

    lax.fori_loop(0, D // many, keep, 0)

    def add(b):
        for k in range(1, F):
            give(b, k).wait_recv()
            out_ref[b] += received[k - 1, b]

    add(d)
    lax.fori_loop(1, D, lambda j, carry: (add(arrival(d, j, D)[0]), carry)[1], 0)

    for c in range(parts):
        for there, by in ((has_left, -1), (has_right, 1)):
            @pl.when(there)
            def _():
                first(by, c).wait_send()

    def drain(j, carry):
        b, to_left = arrival(d, j, D)
        by = 2 * to_left - 1
        onward = jnp.logical_and(d + by >= 0, d + by < D)
        for c in range(parts):
            @pl.when(onward)
            def _():
                along(b, by, c).wait_send()
            for k in range(1, G):
                over(b, k, c).wait_send()
        return carry

    lax.fori_loop(1, D, drain, 0)

    def drain_given(b, carry):
        for k in range(1, F):
            give(b, k).wait_send()
        return carry

    lax.fori_loop(0, D, drain_given, 0)


def local(sizes, train_grads, queries, loss_weights):
    G, D, F = sizes
    total_rows, features = train_grads.shape
    rows = total_rows // F
    parts = 2
    width = features // (G * parts)
    held = queries.shape[1]
    sums = pl.pallas_call(
        functools.partial(kernel, sizes, parts),
        out_shape=jax.ShapeDtypeStruct((D, held, rows), jnp.float32),
        in_specs=[pl.BlockSpec(memory_space=pl.ANY)] * 2,
        out_specs=pl.BlockSpec(memory_space=pltpu.VMEM),
        scratch_shapes=[
            pltpu.VMEM((total_rows, features), jnp.bfloat16),
            pltpu.VMEM((D, G * parts, held, width), jnp.bfloat16),
            pltpu.VMEM((F - 1, D, held, rows), jnp.float32),
            pltpu.VMEM((F - 1, D, held, rows), jnp.float32),
            pltpu.SemaphoreType.DMA((F, G)),
            pltpu.SemaphoreType.DMA((G * parts,)),
            pltpu.SemaphoreType.DMA((2, parts)),
            pltpu.SemaphoreType.DMA((D, parts)),
            pltpu.SemaphoreType.DMA((D, parts)),
            pltpu.SemaphoreType.DMA((D, G, parts)),
            pltpu.SemaphoreType.DMA((D, G, parts)),
            pltpu.SemaphoreType.DMA((D, F - 1)),
            pltpu.SemaphoreType.DMA((D, F - 1)),
        ],
        compiler_params=pltpu.CompilerParams(
            collective_id=0, has_side_effects=True, vmem_limit_bytes=56 * 1024 * 1024
        ),
        cost_estimate=pl.CostEstimate(
            flops=2 * D * held * total_rows * features,
            bytes_accessed=2 * total_rows * features + 4 * D * held * rows,
            transcendentals=0,
        ),
    )(train_grads, queries)
    return sums * loss_weights[None, None, :]


def solution(mesh):
    sizes = tuple(mesh.shape[axis] for axis in ("grp", "dp", "feat"))
    in_specs = (P(("grp", "dp"), "feat"), P("dp", "qry", "feat"), P(("grp", "dp", "feat")))
    out_specs = P(None, "qry", ("grp", "dp", "feat"))
    return jax.shard_map(
        functools.partial(local, sizes), mesh=mesh, in_specs=in_specs, out_specs=out_specs, check_vma=False
    )
```

time: 29.4 us -> 27.4 us (0.932)
  Pallas kernels: 27.4 us -> 25.3 us
    pallas_call x1, Pallas kernels: 27.4 us -> 25.3 us  [local(): pl.pallas_call(functools.partial(kernel, sizes, parts), out_shape=jax.Sha...]
where the time goes in v2:
time: 27.4 us; the launch traced here: 27.2 us
  Pallas kernels  25.3 us (92%)
  other arithmetic  1.84 us (7%)
    pallas_call x1, Pallas kernels, local(): pl.pallas_call(functools.partial(kernel, sizes, parts), out_shape=jax.Sha...  25.3 us
    mul x1, other arithmetic, local(): return sums * loss_weights[None, None, :]  1.84 us

profile of v2, /device:TPU:0, one launch (start us, length us, event | category | flops | bytes accessed | tf_op | source)
XLA Modules:
  0.0 27.2 jit_solution(2077854497106845012)
XLA Ops:
  0.0 0.0 copy-start
  0.0 25.3 %shard_map.37 = f32[4,48,640]{2,1,0:T(8,128)} custom-call(bf16[1280,2048]{1,0:T(8,128)(2,1)} %train_hbm.1, bf16[1,48,2048]{2,1,0:T(8,128)(2,1)} %query_hbm.1), custom_call_target="tpu_custom_call" | custom-call | flops 1006632960 | bytes 5734400 | tf_op jit(solution)/shard_map/pallas_call | solution.py:211
  25.4 0.0 copy-done
  25.4 1.8 %broadcast_multiply_fusion = f32[4,48,640]{2,1,0:T(8,128)} fusion(f32[4,48,640]{2,1,0:T(8,128)} %shard_map.37, f32[640]{0:T(1024)S(1)} %copy-done), kind=kLoop, calls=%fused_computation | loop fusion | flops 122880 | bytes 985600 | tf_op jit(solution)/shard_map/mul | solution.py:240
Async XLA Ops:
  0.0 25.4 %copy-start = (f32[640]{0:T(1024)S(1)}, f32[640]{0:T(1024)}, u32[]{:S(2)}) copy-start(f32[640]{0:T(1024)} %param.5) | copy-start | bytes 7684

commit v3 on v2

--- a/solution.py
+++ b/solution.py
@@ -8,6 +8,9 @@
 from jax.sharding import PartitionSpec as P
 
 MESH = pl.DeviceIdType.MESH
+REACH = 1
+PARTS = 2
+LIMIT = 52
 
 
 def arrival(me, j, size):
@@ -27,11 +30,15 @@
     rows = out_ref.shape[2]
     width = blocks.shape[3]
     pieces = G * parts
-    has_left, has_right = d > 0, d < D - 1
 
     barrier = pltpu.get_barrier_semaphore()
-    for there, by in ((has_left, -1), (has_right, 1)):
-        @pl.when(there)
+    near = [by for t in range(1, min(REACH, D - 1) + 1) for by in (-t, t)]
+
+    def inside(by):
+        return d + by >= 0 if by < 0 else d + by < D
+
+    for by in near:
+        @pl.when(inside(by))
         def _():
             pl.semaphore_signal(barrier, inc=1, device_id={"dp": d + by}, device_id_type=MESH)
     for k in range(1, G):
@@ -54,13 +61,13 @@
             loads.append(pltpu.make_async_copy(train_hbm.at[at], train.at[at], train_sem.at[k, p]))
             loads[-1].start()
 
-    pl.semaphore_wait(barrier, has_left.astype(jnp.int32) + has_right.astype(jnp.int32) + (G - 1) + (F - 1))
+    pl.semaphore_wait(barrier, sum(inside(by).astype(jnp.int32) for by in near) + (G - 1) + (F - 1))
 
     def first(by, c):
         at = pl.multiple_of((g * parts + c) * width, width)
         return pltpu.make_async_remote_copy(
             src_ref=query_hbm.at[0, :, pl.ds(at, width)], dst_ref=blocks.at[d, g * parts + c],
-            send_sem=first_send.at[(by + 1) // 2, c], recv_sem=z_recv.at[d, c],
+            send_sem=first_send.at[near.index(by), c], recv_sem=z_recv.at[d, c],
             device_id={"dp": d + by}, device_id_type=MESH,
         )
 
@@ -85,34 +92,50 @@
             device_id={"grp": lax.rem(g + k, G)}, device_id_type=MESH,
         )
 
-    def give(b, k):
-        return pltpu.make_async_remote_copy(
-            src_ref=sent.at[k - 1, b], dst_ref=received.at[k - 1, b],
-            send_sem=x_send.at[b, k - 1], recv_sem=x_recv.at[b, k - 1],
+    middle = (rows // 128 + 1) // 2 * 128
+    spans = [(0, middle), (middle, rows - middle)] if 0 < middle < rows else [(0, rows)]
+
+    def give(b, k, i):
+        cols = pl.ds(*spans[i])
+        return pltpu.make_async_remote_copy(
+            src_ref=sent.at[k - 1, b, :, cols], dst_ref=received.at[k - 1, b, :, cols],
+            send_sem=x_send.at[b, k - 1, i], recv_sem=x_recv.at[b, k - 1, i],
             device_id={"feat": lax.rem(f + k, F)}, device_id_type=MESH,
         )
 
-    def product(of, k):
-        at = pl.ds(pl.multiple_of(order[k] * rows, rows), rows)
-        total = None
-        for p in range(pieces):
-            term = lax.dot_general(
-                of(p), train[at, pl.ds(p * width, width)],
-                (((1,), (1,)), ((), ())), preferred_element_type=jnp.float32,
-            )
-            total = term if total is None else total + term
-        return total
-
-    def send_products(b):
-        for k in range(1, F):
-            sent[k - 1, b] = product(lambda p: blocks[b, p], k - 1)
-            give(b, k).start()
+    def term(left, p, k, span):
+        at = pl.ds(pl.multiple_of(order[k] * rows + span[0], 16), span[1])
+        cols = pl.ds(pl.multiple_of(p * width, width), width)
+        return lax.dot_general(
+            left, train[at, cols], (((1,), (1,)), ((), ())), preferred_element_type=jnp.float32
+        )
+
+    def product(of, k, span):
+        return functools.reduce(jnp.add, [term(of(p), p, k, span) for p in range(pieces)])
+
+    def send_products(b, waits):
+        at = [(k, i) for k in range(1, F) for i in range(len(spans))]
+        totals = {}
+        for n, wait in enumerate(waits):
+            if wait is not None:
+                wait()
+            p = lax.rem(g + n // parts, G) * parts + n % parts
+            for k, i in at:
+                new = term(blocks[b, p], p, k - 1, spans[i])
+                totals[k, i] = totals[k, i] + new if n else new
+        for k, i in at:
+            sent[k - 1, b, :, pl.ds(*spans[i])] = totals[k, i]
+            give(b, k, i).start()
+
+    def hand_on(b, to_left):
+        by = 2 * to_left - 1
+        far = (d - b) * by >= REACH
+        return by, jnp.logical_and(far, jnp.logical_and(d + by >= 0, d + by < D))
 
     def pass_on(j, c):
         b, to_left = arrival(d, j, D)
         along(b, 1, c).wait_recv()
-        by = 2 * to_left - 1
-        onward = jnp.logical_and(d + by >= 0, d + by < D)
+        by, onward = hand_on(b, to_left)
 
         @pl.when(onward)
         def _():
@@ -122,34 +145,36 @@
 
     def use(j):
         b, _ = arrival(d, j, D)
-        for c in range(parts):
-            for k in range(1, G):
-                over_here(b, k, c).wait_recv()
-        send_products(b)
-
-    for c in range(parts):
-        for there, by in ((has_left, -1), (has_right, 1)):
-            @pl.when(there)
-            def _():
+        waits = [None] * parts
+        for k in range(1, G):
+            waits += [over_here(b, G - k, c).wait_recv for c in range(parts)]
+        send_products(b, waits)
+
+    for by in near:
+        @pl.when(inside(by))
+        def _():
+            for c in range(parts):
                 first(by, c).start()
 
     for copy in own:
         copy.wait()
     for load in loads[: (F - 1) * G]:
         load.wait()
-    send_products(d)
-
-    def step(j):
+    send_products(d, [None] * pieces)
+
+    lag = min(1, D - 1) if D < 3 else jnp.where(jnp.logical_and(d > 0, d < D - 1), 2, 1)
+
+    def step(j, carry):
         for c in range(parts):
-            pass_on(j + 1, c)
-        use(j)
-
-    if D > 1:
-        for c in range(parts):
-            pass_on(1, c)
-        if D > 2:
-            lax.fori_loop(1, D - 1, lambda j, carry: (step(j), carry)[1], 0)
-        use(D - 1)
+            pass_on(j, c)
+
+        @pl.when(j > lag)
+        def _():
+            use(j - lag)
+        return carry
+
+    lax.fori_loop(1, D, step, 0)
+    lax.fori_loop(D - lag, D, lambda j, carry: (use(j), carry)[1], 0)
 
     for load in loads[(F - 1) * G :]:
         load.wait()
@@ -159,7 +184,7 @@
     def keep(i, carry):
         at = pl.ds(i * many, many)
         held = out_ref.shape[1]
-        total = product(lambda p: blocks[at, p].reshape(many * held, width), F - 1)
+        total = product(lambda p: blocks[at, p].reshape(many * held, width), F - 1, (0, rows))
         out_ref[at] = total.reshape(many, held, rows)
         return carry
 
@@ -167,22 +192,22 @@
 
     def add(b):
         for k in range(1, F):
-            give(b, k).wait_recv()
-            out_ref[b] += received[k - 1, b]
+            for i, span in enumerate(spans):
+                give(b, k, i).wait_recv()
+                out_ref[b, :, pl.ds(*span)] += received[k - 1, b, :, pl.ds(*span)]
 
     add(d)
     lax.fori_loop(1, D, lambda j, carry: (add(arrival(d, j, D)[0]), carry)[1], 0)
 
-    for c in range(parts):
-        for there, by in ((has_left, -1), (has_right, 1)):
-            @pl.when(there)
-            def _():
+    for by in near:
+        @pl.when(inside(by))
+        def _():
+            for c in range(parts):
                 first(by, c).wait_send()
 
     def drain(j, carry):
         b, to_left = arrival(d, j, D)
-        by = 2 * to_left - 1
-        onward = jnp.logical_and(d + by >= 0, d + by < D)
+        by, onward = hand_on(b, to_left)
         for c in range(parts):
             @pl.when(onward)
             def _():
@@ -195,7 +220,8 @@
 
     def drain_given(b, carry):
         for k in range(1, F):
-            give(b, k).wait_send()
+            for i in range(len(spans)):
+                give(b, k, i).wait_send()
         return carry
 
     lax.fori_loop(0, D, drain_given, 0)
@@ -205,7 +231,7 @@
     G, D, F = sizes
     total_rows, features = train_grads.shape
     rows = total_rows // F
-    parts = 2
+    parts = PARTS
     width = features // (G * parts)
     held = queries.shape[1]
     sums = pl.pallas_call(
@@ -220,16 +246,16 @@
             pltpu.VMEM((F - 1, D, held, rows), jnp.float32),
             pltpu.SemaphoreType.DMA((F, G)),
             pltpu.SemaphoreType.DMA((G * parts,)),
-            pltpu.SemaphoreType.DMA((2, parts)),
+            pltpu.SemaphoreType.DMA((2 * REACH, parts)),
             pltpu.SemaphoreType.DMA((D, parts)),
             pltpu.SemaphoreType.DMA((D, parts)),
             pltpu.SemaphoreType.DMA((D, G, parts)),
             pltpu.SemaphoreType.DMA((D, G, parts)),
-            pltpu.SemaphoreType.DMA((D, F - 1)),
-            pltpu.SemaphoreType.DMA((D, F - 1)),
+            pltpu.SemaphoreType.DMA((D, F - 1, 2)),
+            pltpu.SemaphoreType.DMA((D, F - 1, 2)),
         ],
         compiler_params=pltpu.CompilerParams(
-            collective_id=0, has_side_effects=True, vmem_limit_bytes=56 * 1024 * 1024
+            collective_id=0, has_side_effects=True, vmem_limit_bytes=LIMIT * 1024 * 1024
         ),
         cost_estimate=pl.CostEstimate(
             flops=2 * D * held * total_rows * features,

time: 27.4 us -> 25.4 us (0.927)
  Pallas kernels: 25.3 us -> 23.4 us
  other arithmetic: 1.84 us -> 0.81 us
  local copies, waits for them, and re-layouts: 0.01 us -> 0.93 us
    pallas_call x1, Pallas kernels: 25.3 us -> 23.4 us  [local(): pl.pallas_call(functools.partial(kernel, sizes, parts), out_shape=jax.Sha...]
    mul x1, other arithmetic: 1.84 us -> 0.81 us  [local(): return sums * loss_weights[None, None, :]]
    unnamed x2 -> x4, local copies, waits for them, and re-layouts: 0.01 us -> 0.93 us
where the time goes in v3:
time: 25.4 us; the launch traced here: 25.2 us
  Pallas kernels  23.4 us (92%)
  local copies, waits for them, and re-layouts  0.93 us (4%)
  other arithmetic  0.81 us (3%)
    pallas_call x1, Pallas kernels, local(): pl.pallas_call(functools.partial(kernel, sizes, parts), out_shape=jax.Sha...  23.4 us
    unnamed x4, local copies, waits for them, and re-layouts  0.93 us
    mul x1, other arithmetic, local(): return sums * loss_weights[None, None, :]  0.81 us

profile of v3, /device:TPU:0, one launch (start us, length us, event | category | flops | bytes accessed | tf_op | source)
XLA Modules:
  0.0 25.2 jit_solution(6894704786827936937)
XLA Ops:
  0.0 0.0 copy-start
  0.0 0.9 %copy-done = bf16[1,48,2048]{2,1,0:T(8,128)(2,1)S(1)} copy-done((bf16[1,48,2048]{2,1,0:T(8,128)(2,1)S(1)}, bf16[1,48,2048]{2,1,0:T(8,128)(2,1)}, u32[]{:S(2)}) %copy-start) | copy-done | bytes 196632
  0.9 0.0 copy-start.1
  0.9 23.4 %shard_map.37 = f32[4,48,640]{2,1,0:T(8,128)S(1)} custom-call(bf16[1280,2048]{1,0:T(8,128)(2,1)} %train_hbm.1, bf16[1,48,2048]{2,1,0:T(8,128)(2,1)S(1)} %copy-done), custom_call_target="tpu_custom_call" | custom-call | flops 1006632960 | bytes 5734400 | tf_op jit(solution)/shard_map/pallas_call | solution.py:237
  24.4 0.0 copy-done.1
  24.4 0.8 %broadcast_multiply_fusion = f32[4,48,640]{2,1,0:T(8,128)} fusion(f32[4,48,640]{2,1,0:T(8,128)S(1)} %shard_map.37, f32[640]{0:T(1024)S(1)} %copy-done.1), kind=kLoop, calls=%fused_computation | loop fusion | flops 122880 | bytes 985600 | tf_op jit(solution)/shard_map/mul | solution.py:266
Async XLA Ops:
  0.0 0.9 %copy-start = (bf16[1,48,2048]{2,1,0:T(8,128)(2,1)S(1)}, bf16[1,48,2048]{2,1,0:T(8,128)(2,1)}, u32[]{:S(2)}) copy-start(bf16[1,48,2048]{2,1,0:T(8,128)(2,1)} %query_hbm.1) | copy-start | bytes 589828
  0.9 23.5 %copy-start.1 = (f32[640]{0:T(1024)S(1)}, f32[640]{0:T(1024)}, u32[]{:S(2)}) copy-start(f32[640]{0:T(1024)} %param.5) | copy-start | bytes 7684

commit v4 on v3

--- a/solution.py
+++ b/solution.py
@@ -8,17 +8,8 @@
 from jax.sharding import PartitionSpec as P
 
 MESH = pl.DeviceIdType.MESH
-REACH = 1
 PARTS = 2
 LIMIT = 52
-
-
-def arrival(me, j, size):
-    both = jnp.minimum(me, size - 1 - me)
-    left_longer = (2 * me) // size
-    step = jnp.where(j <= 2 * both, (j + 1) // 2, j - both)
-    to_left = jnp.where(j <= 2 * both, j % 2, left_longer)
-    return me + step * (1 - 2 * to_left), to_left
 
 
 def kernel(
@@ -32,7 +23,7 @@
     pieces = G * parts
 
     barrier = pltpu.get_barrier_semaphore()
-    near = [by for t in range(1, min(REACH, D - 1) + 1) for by in (-t, t)]
+    near = (-1, 1)
 
     def inside(by):
         return d + by >= 0 if by < 0 else d + by < D
@@ -127,24 +118,22 @@
             sent[k - 1, b, :, pl.ds(*spans[i])] = totals[k, i]
             give(b, k, i).start()
 
-    def hand_on(b, to_left):
-        by = 2 * to_left - 1
-        far = (d - b) * by >= REACH
-        return by, jnp.logical_and(far, jnp.logical_and(d + by >= 0, d + by < D))
-
-    def pass_on(j, c):
-        b, to_left = arrival(d, j, D)
-        along(b, 1, c).wait_recv()
-        by, onward = hand_on(b, to_left)
-
-        @pl.when(onward)
+    def both_sides(t, act):
+        for by in (1, -1):
+            @pl.when(d - t * by >= 0 if by > 0 else d - t * by < D)
+            def _():
+                act(d - t * by, by)
+
+    def pass_on(b, by, c):
+        along(b, by, c).wait_recv()
+
+        @pl.when(inside(by))
         def _():
             along(b, by, c).start()
         for k in range(1, G):
             over(b, k, c).start()
 
-    def use(j):
-        b, _ = arrival(d, j, D)
+    def use(b):
         waits = [None] * parts
         for k in range(1, G):
             waits += [over_here(b, G - k, c).wait_recv for c in range(parts)]
@@ -162,19 +151,18 @@
         load.wait()
     send_products(d, [None] * pieces)
 
-    lag = min(1, D - 1) if D < 3 else jnp.where(jnp.logical_and(d > 0, d < D - 1), 2, 1)
-
-    def step(j, carry):
+    def step(t, carry):
         for c in range(parts):
-            pass_on(j, c)
-
-        @pl.when(j > lag)
-        def _():
-            use(j - lag)
+            both_sides(t, lambda b, by: pass_on(b, by, c))
+
+        @pl.when(t > 1)
+        def _():
+            both_sides(t - 1, lambda b, by: use(b))
         return carry
 
     lax.fori_loop(1, D, step, 0)
-    lax.fori_loop(D - lag, D, lambda j, carry: (use(j), carry)[1], 0)
+    if D > 1:
+        both_sides(D - 1, lambda b, by: use(b))
 
     for load in loads[(F - 1) * G :]:
         load.wait()
@@ -197,7 +185,7 @@
                 out_ref[b, :, pl.ds(*span)] += received[k - 1, b, :, pl.ds(*span)]
 
     add(d)
-    lax.fori_loop(1, D, lambda j, carry: (add(arrival(d, j, D)[0]), carry)[1], 0)
+    lax.fori_loop(1, D, lambda t, carry: (both_sides(t, lambda b, by: add(b)), carry)[1], 0)
 
     for by in near:
         @pl.when(inside(by))
@@ -205,18 +193,15 @@
             for c in range(parts):
                 first(by, c).wait_send()
 
-    def drain(j, carry):
-        b, to_left = arrival(d, j, D)
-        by, onward = hand_on(b, to_left)
+    def left(b, by):
         for c in range(parts):
-            @pl.when(onward)
+            @pl.when(inside(by))
             def _():
                 along(b, by, c).wait_send()
             for k in range(1, G):
                 over(b, k, c).wait_send()
-        return carry
-
-    lax.fori_loop(1, D, drain, 0)
+
+    lax.fori_loop(1, D, lambda t, carry: (both_sides(t, left), carry)[1], 0)
 
     def drain_given(b, carry):
         for k in range(1, F):
@@ -246,7 +231,7 @@
             pltpu.VMEM((F - 1, D, held, rows), jnp.float32),
             pltpu.SemaphoreType.DMA((F, G)),
             pltpu.SemaphoreType.DMA((G * parts,)),
-            pltpu.SemaphoreType.DMA((2 * REACH, parts)),
+            pltpu.SemaphoreType.DMA((2, parts)),
             pltpu.SemaphoreType.DMA((D, parts)),
             pltpu.SemaphoreType.DMA((D, parts)),
             pltpu.SemaphoreType.DMA((D, G, parts)),

time: 25.4 us -> 24.7 us (0.972)
  Pallas kernels: 23.4 us -> 22.8 us
    pallas_call x1, Pallas kernels: 23.4 us -> 22.8 us  [local(): pl.pallas_call(functools.partial(kernel, sizes, parts), out_shape=jax.Sha...]
where the time goes in v4:
time: 24.7 us; the launch traced here: 24.6 us
  Pallas kernels  22.8 us (92%)
  local copies, waits for them, and re-layouts  0.93 us (4%)
  other arithmetic  0.81 us (3%)
    pallas_call x1, Pallas kernels, local(): pl.pallas_call(functools.partial(kernel, sizes, parts), out_shape=jax.Sha...  22.8 us
    unnamed x4, local copies, waits for them, and re-layouts  0.93 us
    mul x1, other arithmetic, local(): return sums * loss_weights[None, None, :]  0.81 us

profile of v4, /device:TPU:0, one launch (start us, length us, event | category | flops | bytes accessed | tf_op | source)
XLA Modules:
  0.0 24.6 jit_solution(6110510128580995477)
XLA Ops:
  0.0 0.0 copy-start
  0.0 0.9 %copy-done = bf16[1,48,2048]{2,1,0:T(8,128)(2,1)S(1)} copy-done((bf16[1,48,2048]{2,1,0:T(8,128)(2,1)S(1)}, bf16[1,48,2048]{2,1,0:T(8,128)(2,1)}, u32[]{:S(2)}) %copy-start) | copy-done | bytes 196632
  0.9 0.0 copy-start.1
  0.9 22.8 %shard_map.37 = f32[4,48,640]{2,1,0:T(8,128)S(1)} custom-call(bf16[1280,2048]{1,0:T(8,128)(2,1)} %train_hbm.1, bf16[1,48,2048]{2,1,0:T(8,128)(2,1)S(1)} %copy-done), custom_call_target="tpu_custom_call" | custom-call | flops 1006632960 | bytes 5734400 | tf_op jit(solution)/shard_map/pallas_call | solution.py:222
  23.8 0.0 copy-done.1
  23.8 0.8 %broadcast_multiply_fusion = f32[4,48,640]{2,1,0:T(8,128)} fusion(f32[4,48,640]{2,1,0:T(8,128)S(1)} %shard_map.37, f32[640]{0:T(1024)S(1)} %copy-done.1), kind=kLoop, calls=%fused_computation | loop fusion | flops 122880 | bytes 985600 | tf_op jit(solution)/shard_map/mul | solution.py:251
Async XLA Ops:
  0.0 0.9 %copy-start = (bf16[1,48,2048]{2,1,0:T(8,128)(2,1)S(1)}, bf16[1,48,2048]{2,1,0:T(8,128)(2,1)}, u32[]{:S(2)}) copy-start(bf16[1,48,2048]{2,1,0:T(8,128)(2,1)} %query_hbm.1) | copy-start | bytes 589828
  0.9 22.8 %copy-start.1 = (f32[640]{0:T(1024)S(1)}, f32[640]{0:T(1024)}, u32[]{:S(2)}) copy-start(f32[640]{0:T(1024)} %param.5) | copy-start | bytes 7684

commit v5 on v4

--- a/solution.py
+++ b/solution.py
@@ -114,9 +114,9 @@
             for k, i in at:
                 new = term(blocks[b, p], p, k - 1, spans[i])
                 totals[k, i] = totals[k, i] + new if n else new
-        for k, i in at:
-            sent[k - 1, b, :, pl.ds(*spans[i])] = totals[k, i]
-            give(b, k, i).start()
+                if n == len(waits) - 1:
+                    sent[k - 1, b, :, pl.ds(*spans[i])] = totals[k, i]
+                    give(b, k, i).start()
 
     def both_sides(t, act):
         for by in (1, -1):

time: 24.7 us -> 24.7 us (level)
  no operation moved by 1% of the time
where the time goes in v5:
time: 24.7 us; the launch traced here: 24.6 us
  Pallas kernels  22.8 us (92%)
  local copies, waits for them, and re-layouts  0.93 us (4%)
  other arithmetic  0.81 us (3%)
    pallas_call x1, Pallas kernels, local(): pl.pallas_call(functools.partial(kernel, sizes, parts), out_shape=jax.Sha...  22.8 us
    unnamed x4, local copies, waits for them, and re-layouts  0.93 us
    mul x1, other arithmetic, local(): return sums * loss_weights[None, None, :]  0.81 us

profile of v5, /device:TPU:0, one launch (start us, length us, event | category | flops | bytes accessed | tf_op | source)
XLA Modules:
  0.0 24.6 jit_solution(13449421330746977337)
XLA Ops:
  0.0 0.0 copy-start
  0.0 0.9 %copy-done = bf16[1,48,2048]{2,1,0:T(8,128)(2,1)S(1)} copy-done((bf16[1,48,2048]{2,1,0:T(8,128)(2,1)S(1)}, bf16[1,48,2048]{2,1,0:T(8,128)(2,1)}, u32[]{:S(2)}) %copy-start) | copy-done | bytes 196632
  0.9 0.0 copy-start.1
  0.9 22.8 %shard_map.37 = f32[4,48,640]{2,1,0:T(8,128)S(1)} custom-call(bf16[1280,2048]{1,0:T(8,128)(2,1)} %train_hbm.1, bf16[1,48,2048]{2,1,0:T(8,128)(2,1)S(1)} %copy-done), custom_call_target="tpu_custom_call" | custom-call | flops 1006632960 | bytes 5734400 | tf_op jit(solution)/shard_map/pallas_call | solution.py:222
  23.8 0.0 copy-done.1
  23.8 0.8 %broadcast_multiply_fusion = f32[4,48,640]{2,1,0:T(8,128)} fusion(f32[4,48,640]{2,1,0:T(8,128)S(1)} %shard_map.37, f32[640]{0:T(1024)S(1)} %copy-done.1), kind=kLoop, calls=%fused_computation | loop fusion | flops 122880 | bytes 985600 | tf_op jit(solution)/shard_map/mul | solution.py:251
Async XLA Ops:
  0.0 0.9 %copy-start = (bf16[1,48,2048]{2,1,0:T(8,128)(2,1)S(1)}, bf16[1,48,2048]{2,1,0:T(8,128)(2,1)}, u32[]{:S(2)}) copy-start(bf16[1,48,2048]{2,1,0:T(8,128)(2,1)} %query_hbm.1) | copy-start | bytes 589828
  0.9 22.8 %copy-start.1 = (f32[640]{0:T(1024)S(1)}, f32[640]{0:T(1024)}, u32[]{:S(2)}) copy-start(f32[640]{0:T(1024)} %param.5) | copy-start | bytes 7684
